TPU v7x, 32 devices: a whole 2x2x4 slice. The times are simulated.
32 devices in a mesh: grp: 2 (over y), ctx: 8 (over z, core), dp: 2 (over x).
Axes of the slice: x: 2, y: 2, z: 4, core: 2. Of those that a mesh axis runs over, the one named last changes fastest.
Arguments:
- resid: bfloat16 [2, 1024, 1024], P('dp', 'ctx'), may hold values from -6 to 6
- attn_ctx: bfloat16 [2, 1024, 1024], P('dp', 'ctx', 'grp'), may hold values from -6 to 6
- enc_out_weight: bfloat16 [1024, 1024], P('grp'), may hold values from -0.1875 to 0.1875
- enc_gain: bfloat16 [1024], replicated, may hold values from 0.25 to 1.75
- key_weight: bfloat16 [1024, 1024], P(None, 'grp'), may hold values from -0.1875 to 0.1875
- value_weight: bfloat16 [1024, 1024], P(None, 'grp'), may hold values from -0.1875 to 0.1875
- visual_grad: bfloat16 [2, 1024, 1024], P('dp', 'ctx'), may hold values from -6 to 6
- scene_lengths: int32 [2, 4], P('dp'), may hold values from 1 to 384, 1024 in all within a row
- text_queries: bfloat16 [2, 1280, 4096], P('dp', 'ctx', 'grp'), may hold values from -86 to 86
- text_segments: int32 [2, 1280], P('dp', 'ctx'), may hold values from 0 to 7, never falling along the last dimension, each value on 1 to 320 neighbouring positions
- doc_scene: int32 [2, 8], P('dp'), may hold values from 0 to 3
Outputs:
- cross_context: bfloat16 [2, 1280, 4096], P('dp', 'ctx', 'grp')
- enc_out_grad: float32 [1024, 1024], P(('grp', 'ctx'))
Inputs may be any that keep to these rules, and one draw needn't show every extreme that they name: `scene_lengths`: each replica's counts sum to 1024; the largest is exactly the maximum. `text_segments`: never falling along a sequence.
All inputs are finite; a program needn't handle non-finite values.
Results may differ from a plain program's by a relative error of at most 0.025.
Values may be sent and summed in bfloat16 or wider, within the bound.
A program may use at most 64 MiB of HBM per device.

v0:
```python
import math

import jax
import jax.numpy as jnp
from jax import lax
from jax.sharding import PartitionSpec as P

Q_HEADS = 32
KV_HEADS = 8
HEAD_DIM = 128


NEGATIVE = -1e30
EPSILON = 1e-05


def scene_index(lengths, first_row, count):
    scene_ends = jnp.cumsum(lengths)
    position = first_row + jnp.arange(count, dtype=jnp.int32)
    return jnp.sum((position[:, None] >= scene_ends[None, :]).astype(jnp.int32), axis=1)


def query_scenes(segments, doc_scene):
    doc_numbers = jnp.arange(doc_scene.shape[0], dtype=jnp.int32)
    picked = (segments[:, None] == doc_numbers[None, :]).astype(jnp.int32)
    return jnp.sum(picked * doc_scene[None, :], axis=1)


def normalize(hidden, enc_gain):
    root_mean = jnp.sqrt(jnp.mean(hidden * hidden, axis=-1, keepdims=True) + EPSILON)
    normed = hidden / root_mean
    visual = (normed * enc_gain.astype(jnp.float32)).astype(jnp.bfloat16)
    return (normed, root_mean, visual)


def norm_backward(cotangent, normed, root_mean, enc_gain):
    upstream = cotangent.astype(jnp.float32) * enc_gain.astype(jnp.float32)
    inner = jnp.mean(upstream * normed, axis=-1, keepdims=True)
    return ((upstream - normed * inner) / root_mean).astype(jnp.bfloat16)


def local(
    resid,
    attn_ctx,
    enc_out_weight,
    enc_gain,
    key_weight,
    value_weight,
    visual_grad,
    scene_lengths,
    text_queries,
    text_segments,
    doc_scene,
):
    context_rows = attn_ctx[0]
    partial_value = jnp.dot(context_rows, enc_out_weight, preferred_element_type=jnp.float32)
    summed = lax.psum(partial_value, "grp")
    hidden = resid[0].astype(jnp.float32) + summed
    normed, root_mean, visual = normalize(hidden, enc_gain)
    key_rows = jnp.dot(visual, key_weight, preferred_element_type=jnp.float32).astype(jnp.bfloat16)
    value_rows = jnp.dot(visual, value_weight, preferred_element_type=jnp.float32).astype(
        jnp.bfloat16
    )
    group_size = Q_HEADS // KV_HEADS
    kv_local = key_rows.shape[1] // HEAD_DIM
    text_count = text_queries.shape[1]
    queries = text_queries[0].reshape(text_count, kv_local, group_size, HEAD_DIM)
    query_scene = query_scenes(text_segments[0], doc_scene[0])
    lengths = scene_lengths[0]
    scale = HEAD_DIM ** (-0.5)

    def absorb(carry, block_keys, block_values, first_row):
        count = block_keys.shape[0]
        key_scene = scene_index(lengths, first_row, count)
        allowed = (query_scene[:, None] == key_scene[None, :])[None, None]
        run_max, run_total, run_acc = carry
        key_mat = block_keys.reshape(count, kv_local, HEAD_DIM)
        value_mat = block_values.reshape(count, kv_local, HEAD_DIM)
        scores = (
            jnp.einsum("tkgd,skd->kgts", queries, key_mat, preferred_element_type=jnp.float32)
            * scale
        )
        scores = jnp.where(allowed, scores, NEGATIVE)
        new_max = jnp.maximum(run_max, jnp.max(scores, axis=-1))
        weights = jnp.where(allowed, jnp.exp(scores - new_max[..., None]), 0.0).astype(jnp.bfloat16)
        factor = jnp.exp(run_max - new_max)
        new_total = run_total * factor + jnp.sum(weights.astype(jnp.float32), axis=-1)
        new_acc = run_acc * factor[..., None] + jnp.einsum(
            "kgts,skd->kgtd", weights, value_mat, preferred_element_type=jnp.float32
        )
        return (new_max, new_total, new_acc)

    start_state = (
        jnp.full((kv_local, group_size, text_count), NEGATIVE, jnp.float32),
        jnp.zeros((kv_local, group_size, text_count), jnp.float32),
        jnp.zeros((kv_local, group_size, text_count, HEAD_DIM), jnp.float32),
    )
    shard_keys = lax.all_gather(key_rows, "ctx", axis=0, tiled=True)
    shard_values = lax.all_gather(value_rows, "ctx", axis=0, tiled=True)
    count = shard_keys.shape[0]
    block = math.gcd(count, 512)

    def turn_step(turn, inner):
        offset = turn * block
        block_keys = lax.dynamic_slice_in_dim(shard_keys, offset, block, 0)
        block_values = lax.dynamic_slice_in_dim(shard_values, offset, block, 0)
        return absorb(inner, block_keys, block_values, offset)

    final_max, final_total, final_acc = lax.fori_loop(0, count // block, turn_step, start_state)
    attended = final_acc / final_total[..., None]
    cross_context = (
        jnp.transpose(attended, (2, 0, 1, 3))
        .reshape(1, text_count, kv_local * group_size * HEAD_DIM)
        .astype(jnp.bfloat16)
    )
    hidden_grad = norm_backward(visual_grad[0], normed, root_mean, enc_gain)
    weight_term = lax.dot_general(
        context_rows, hidden_grad, (((0,), (0,)), ((), ())), preferred_element_type=jnp.float32
    )
    replica_total = lax.psum(weight_term.astype(jnp.bfloat16), "dp")
    weight_grad = lax.psum_scatter(replica_total, "ctx", scatter_dimension=0, tiled=True).astype(
        jnp.float32
    )
    return (cross_context, weight_grad)


def solution(mesh):
    in_specs = (
        P("dp", "ctx", None),
        P("dp", "ctx", "grp"),
        P("grp", None),
        P(),
        P(None, "grp"),
        P(None, "grp"),
        P("dp", "ctx", None),
        P("dp", None),
        P("dp", "ctx", "grp"),
        P("dp", "ctx"),
        P("dp", None),
    )
    out_specs = (P("dp", "ctx", "grp"), P(("grp", "ctx"), None))
    return jax.shard_map(local, mesh=mesh, in_specs=in_specs, out_specs=out_specs, check_vma=False)
```

profile of v0, /device:TPU:0, one launch (start us, length us, event | category | flops | bytes accessed | tf_op | source)
XLA Modules:
  0.0 159.2 jit_solution(17036779635868595269)
XLA Ops:
  7.2 0.0 copy-start
  7.2 0.0 copy-start.4
  7.2 0.0 copy-start.13
  7.2 0.0 copy-start.5
  7.2 0.0 all-reduce.3.cloned.1.call-start
  7.3 1.1 copy-done
  8.4 2.0 %fusion.16 = f32[128,1024]{1,0:T(8,128)} fusion(bf16[512,1024]{1,0:T(8,128)(2,1)S(1)} %copy-done, bf16[1,128,512]{2,1,0:T(8,128)(2,1)} %param.14), kind=kOutput, calls=%fused_computation.36 | convolution fusion | flops 134217728 | bytes 1703936 | tf_op jit(solution)/shard_map/dot_general | solution.py:56
  10.4 0.0 all-reduce.3.cloned.1.call-update
  10.4 0.0 all-gather.5.cloned.1.call-start
  10.5 0.7 convert_element_type.84
  11.2 31.0 %all-reduce.3.cloned.1.call-done = f32[128,1024]{1,0:T(8,128)} async-done(((f32[128,1024]{1,0:T(8,128)}), f32[128,1024]{1,0:T(8,128)}) %all-reduce.3.cloned.1.call-update) | async-done | bytes 524304 | tf_op jit(solution)/shard_map/psum | solution.py:57
  42.2 1.3 multiply_reduce_fusion
  43.6 2.5 %convolution_convert_fusion.1 = bf16[128,512]{1,0:T(8,128)(2,1)} fusion(bf16[1024,512]{1,0:T(8,128)(2,1)} %param.18, f32[1024]{0:T(1024)S(1)} %convert_element_type.84, f32[128,1024]{1,0:T(8,128)} %all-reduce.3.cloned.1.call-done, bf16[1,128,1024]{2,1,0:T(8,128)(2,1)} %param.13, f32[128]{0:T(128)S(1)} %add_sqrt_fusion), kind=kOutput, calls=%fused_computation.18 | convolution fusion | flops 134938624 | bytes 1970688 | tf_op jit(solution)/shard_map/dot_general | solution.py:61
  46.1 0.0 all-gather.5.cloned.1.call-update
  46.1 0.0 all-gather.3.cloned.1.call-start
  46.1 0.0 copy-done.4
  46.2 2.4 %convolution_convert_fusion.2 = bf16[128,512]{1,0:T(8,128)(2,1)} fusion(bf16[1024,512]{1,0:T(8,128)(2,1)} %param.17, f32[1024]{0:T(1024)S(1)} %convert_element_type.84, f32[128,1024]{1,0:T(8,128)} %all-reduce.3.cloned.1.call-done, bf16[1,128,1024]{2,1,0:T(8,128)(2,1)S(1)} %copy-done.4, f32[128]{0:T(128)S(1)} %add_sqrt_fusion), kind=kOutput, calls=%fused_computation.19 | convolution fusion | flops 134938624 | bytes 1970688 | tf_op jit(solution)/shard_map/dot_general | solution.py:60
  48.6 0.0 all-gather.3.cloned.1.call-update
  48.6 0.0 reduce-scatter.4.cloned.1.call-start
  48.7 0.0 copy-done.13
  48.7 0.8 broadcast_in_dim.86
  49.4 0.0 copy-done.5
  49.4 0.5 reshape_squeeze.3
  49.9 0.2 copy.32
  50.1 0.0 copy-done.10
  50.1 0.0 copy-done.12
  50.1 0.7 select_reduce_fusion
  50.8 0.0 copy-done.8
  50.8 0.2 fusion.6
  51.0 1.5 fusion.2
  52.6 1.3 copy.42
  53.9 0.0 reduce-scatter.4.cloned.1.call-update
  53.9 0.0 all-reduce.5.cloned.1.call-start
  53.9 14.4 %all-gather.5.cloned.1.call-done = bf16[1024,512]{1,0:T(8,128)(2,1)} async-done(((bf16[128,512]{1,0:T(8,128)(2,1)}), bf16[1024,512]{1,0:T(8,128)(2,1)}) %all-gather.5.cloned.1.call-update) | async-done | bytes 1048592 | tf_op jit(solution)/shard_map/all_gather | solution.py:99
  68.3 24.0 %all-gather.3.cloned.1.call-done = bf16[1024,512]{1,0:T(8,128)(2,1)} async-done(((bf16[128,512]{1,0:T(8,128)(2,1)}), bf16[1024,512]{1,0:T(8,128)(2,1)}) %all-gather.3.cloned.1.call-update) | async-done | bytes 1048592 | tf_op jit(solution)/shard_map/all_gather | solution.py:98
  92.4 18.9 %while.20 = (s32[]{:T(128)}, f32[4,4,160]{2,1,0:T(4,128)S(1)}, f32[4,4,160]{2,1,0:T(4,128)}, f32[4,4,160,128]{3,2,1,0:T(8,128)}, s32[160]{0:T(256)}, /*index=5*/...) while((s32[]{:T(128)}, f32[4,4,160]{2,1,0:T(4,128)S(1)}, ...), condition=%wide.region_8.9_spmd.clone, body=%wide.region_4.8_spmd.clone.sunk | while | flops 691833344 | bytes 35316676 | solution.py:109
  92.4 0.7 convert_reduce_fusion.4
  93.1 0.8 broadcast_compare_fusion.2
  93.9 1.3 constant_dynamic-slice_fusion.3
  95.2 0.2 copy.48
  95.4 0.2 copy.49
  95.6 1.1 fusion.35
  96.8 1.9 %convert_reduce_fusion.5 = f32[4,4,160]{2,1,0:T(4,128)S(1)} fusion(f32[4,4,160]{2,1,0:T(4,128)S(1)} %select_maximum_fusion.2, f32[4,512,160,4]{1,2,3,0:T(8,128)S(1)} %get-tuple-element.369, pred[160,512]{1,0:T(8,128)(4,1)S(1)} %broadcast_compare_fusion.2), kind=kLoop, calls=%fused_computation.1.clone.1 | loop fusion | flops 9172480 | bytes 5345280 | tf_op jit(solution)/shard_map/while/body/eval_jaxpr/reduce_sum | solution.py:87
  98.7 2.0 %convolution_add_fusion.2 = f32[4,4,160,128]{3,2,1,0:T(8,128)S(1)} fusion(bf16[512,4,128,1]{0,2,3,1:T(8,128)(2,1)S(1)} %bitcast.79, f32[4,4,160,128]{3,2,1,0:T(8,128)S(1)} %copy-done.2, f32[4,4,160]{2,1,0:T(4,128)S(1)} %get-tuple-element.372, pred[]{:T(512)S(6)} %compare.3, f32[4,512,160,4]{1,2,3,0:T(8,128)S(1)} %get-tuple-element.369, ...), kind=kOutput, calls=%fused_computation.4.clone.1 | convolution fusion | flops 343080960 | bytes 8491009 | tf_op jit(solution)/shard_map/while/body/eval_jaxpr/kgts,skd->kgtd/dot_general | solution.py:88
  100.8 1.0 copy-done.3
  101.8 0.7 convert_reduce_fusion.4
  102.6 0.8 broadcast_compare_fusion.2
  103.4 1.3 constant_dynamic-slice_fusion.3
  104.6 0.2 copy.48
  104.9 0.2 copy.49
  105.1 0.0 copy-start.6
  105.1 0.0 copy-start.2
  105.1 1.1 fusion.35
  106.2 1.9 %convert_reduce_fusion.5 = f32[4,4,160]{2,1,0:T(4,128)S(1)} fusion(f32[4,4,160]{2,1,0:T(4,128)S(1)} %select_maximum_fusion.2, f32[4,512,160,4]{1,2,3,0:T(8,128)S(1)} %get-tuple-element.369, pred[160,512]{1,0:T(8,128)(4,1)S(1)} %broadcast_compare_fusion.2), kind=kLoop, calls=%fused_computation.1.clone.1 | loop fusion | flops 9172480 | bytes 5345280 | tf_op jit(solution)/shard_map/while/body/eval_jaxpr/reduce_sum | solution.py:87
  108.2 2.0 %convolution_add_fusion.2 = f32[4,4,160,128]{3,2,1,0:T(8,128)S(1)} fusion(bf16[512,4,128,1]{0,2,3,1:T(8,128)(2,1)S(1)} %bitcast.79, f32[4,4,160,128]{3,2,1,0:T(8,128)S(1)} %copy-done.2, f32[4,4,160]{2,1,0:T(4,128)S(1)} %get-tuple-element.372, pred[]{:T(512)S(6)} %compare.3, f32[4,512,160,4]{1,2,3,0:T(8,128)S(1)} %get-tuple-element.369, ...), kind=kOutput, calls=%fused_computation.4.clone.1 | convolution fusion | flops 343080960 | bytes 8491009 | tf_op jit(solution)/shard_map/while/body/eval_jaxpr/kgts,skd->kgtd/dot_general | solution.py:88
  110.2 1.0 copy-done.3
  111.3 15.3 %reduce-scatter.4.cloned.1.call-done = bf16[64,1024]{1,0:T(8,128)(2,1)} async-done(((bf16[512,1024]{1,0:T(8,128)(2,1)}), bf16[64,1024]{1,0:T(8,128)(2,1)}) %reduce-scatter.4.cloned.1.call-update) | async-done | bytes 131088
  126.6 1.7 %copy.43 = bf16[64,1024]{0,1:T(8,128)(2,1)} copy(bf16[64,1024]{1,0:T(8,128)(2,1)} %reduce-scatter.4.cloned.1.call-done) | data formatting | bytes 262144
  128.3 0.0 all-reduce.5.cloned.1.call-update
  128.4 1.7 %fusion.3 = bf16[160,4,4,128]{3,0,2,1:T(8,128)(2,1)S(1)} fusion(f32[4,4,160,128]{3,2,1,0:T(8,128)} %get-tuple-element.215, f32[4,4,160]{2,1,0:T(4,128)} %get-tuple-element.216), kind=kLoop, calls=%fused_computation.20 | loop fusion | flops 655360 | bytes 1976320 | tf_op jit(solution)/shard_map/convert_element_type | solution.py:114
  130.1 0.3 copy.34
  130.5 1.3 convert_element_type.90
  131.8 19.1 %all-reduce.5.cloned.1.call-done = bf16[64,1024]{0,1:T(8,128)(2,1)} async-done(((bf16[64,1024]{0,1:T(8,128)(2,1)}), bf16[64,1024]{0,1:T(8,128)(2,1)}) %all-reduce.5.cloned.1.call-update) | async-done | bytes 131088 | tf_op jit(solution)/shard_map/psum | solution.py:120
  150.9 1.8 %copy.35 = f32[64,1024]{1,0:T(8,128)} copy(bf16[64,1024]{0,1:T(8,128)(2,1)} %all-reduce.5.cloned.1.call-done) | data formatting | bytes 393216
  (34 shorter events, 0.1 us)
Async XLA Ops:
  7.2 1.2 copy-start
  7.2 39.0 %copy-start.4 = (bf16[1,128,1024]{2,1,0:T(8,128)(2,1)S(1)}, bf16[1,128,1024]{2,1,0:T(8,128)(2,1)}, u32[]{:S(2)}) copy-start(bf16[1,128,1024]{2,1,0:T(8,128)(2,1)} %param.13) | copy-start | bytes 786436
  7.2 41.5 %copy-start.13 = (s32[1,4]{1,0:T(1,128)S(1)}, s32[1,4]{1,0:T(1,128)}, u32[]{:S(2)}) copy-start(s32[1,4]{1,0:T(1,128)} %param.20) | copy-start | bytes 52
  7.2 42.2 %copy-start.5 = (bf16[1,160,2048]{2,1,0:T(8,128)(2,1)S(1)}, bf16[1,160,2048]{2,1,0:T(8,128)(2,1)}, u32[]{:S(2)}) copy-start(bf16[1,160,2048]{2,1,0:T(8,128)(2,1)} %param.21) | copy-start | bytes 1966084
  7.2 35.0 %all-reduce.3.cloned.1.call-start = ((), (), s32[]{:S(2)}) async-start(), calls=%async_computation.1 | async-start | bytes 1048576 | tf_op jit(solution)/shard_map/psum | solution.py:57
  10.4 39.7 %copy-start.10 = (s32[1,160]{1,0:T(1,128)S(1)}, s32[1,160]{1,0:T(1,128)}, u32[]{:S(2)}) copy-start(s32[1,160]{1,0:T(1,128)} %param.22) | copy-start | bytes 1924
  10.4 39.7 %copy-start.12 = (s32[1,8]{1,0:T(1,128)S(1)}, s32[1,8]{1,0:T(1,128)}, u32[]{:S(2)}) copy-start(s32[1,8]{1,0:T(1,128)} %param.23) | copy-start | bytes 100
  10.4 40.3 %copy-start.8 = (bf16[1,128,1024]{2,1,0:T(8,128)(2,1)S(1)}, bf16[1,128,1024]{2,1,0:T(8,128)(2,1)}, u32[]{:S(2)}) copy-start(bf16[1,128,1024]{2,1,0:T(8,128)(2,1)} %param.19) | copy-start | bytes 786436
  10.4 57.9 %all-gather.5.cloned.1.call-start = ((), (), s32[]{:S(2)}) async-start(), calls=%async_computation.3 | async-start | bytes 1179648 | tf_op jit(solution)/shard_map/all_gather | solution.py:99
  11.2 39.8 %copy-start.9 = (f32[1024]{0:T(1024)}, f32[1024]{0:T(1024)S(1)}, u32[]{:S(2)}) copy-start(f32[1024]{0:T(1024)S(1)} %convert_element_type.84) | copy-start | bytes 12292
  42.2 8.5 %copy-start.1 = (f32[128,1024]{1,0:T(8,128)S(1)}, f32[128,1024]{1,0:T(8,128)}, u32[]{:S(2)}) copy-start(f32[128,1024]{1,0:T(8,128)} %all-reduce.3.cloned.1.call-done) | copy-start | bytes 1572868
  43.6 7.4 %copy-start.11 = (f32[128]{0:T(128)}, f32[128]{0:T(128)S(1)}, u32[]{:S(2)}) copy-start(f32[128]{0:T(128)S(1)} %add_sqrt_fusion) | copy-start | bytes 1540
  46.1 46.3 %all-gather.3.cloned.1.call-start = ((), (), s32[]{:S(2)}) async-start(), calls=%async_computation.2 | async-start | bytes 1179648 | tf_op jit(solution)/shard_map/all_gather | solution.py:98
  48.6 78.0 %reduce-scatter.4.cloned.1.call-start = ((), (), s32[]{:S(2)}) async-start(), calls=%async_computation.5 | async-start | bytes 1179648
  53.9 97.0 %all-reduce.5.cloned.1.call-start = ((), (), s32[]{:S(2)}) async-start(), calls=%async_computation.4 | async-start | bytes 524288 | tf_op jit(solution)/shard_map/psum | solution.py:120
  95.6 3.0 %copy-start.6 = (f32[4,4,160]{2,1,0:T(4,128)S(1)}, f32[4,4,160]{2,1,0:T(4,128)}, u32[]{:S(2)}) copy-start(f32[4,4,160]{2,1,0:T(4,128)} %get-tuple-element.388) | copy-start | bytes 30724 | tf_op jit(solution)/shard_map/while
  95.6 3.1 %copy-start.2 = (f32[4,4,160,128]{3,2,1,0:T(8,128)S(1)}, f32[4,4,160,128]{3,2,1,0:T(8,128)}, u32[]{:S(2)}) copy-start(f32[4,4,160,128]{3,2,1,0:T(8,128)} %get-tuple-element.389) | copy-start | bytes 3932164 | tf_op jit(solution)/shard_map/while
  98.7 2.1 %copy-start.7 = (f32[4,4,160]{2,1,0:T(4,128)}, f32[4,4,160]{2,1,0:T(4,128)S(1)}, u32[]{:S(2)}) copy-start(f32[4,4,160]{2,1,0:T(4,128)S(1)} %get-tuple-element.401) | copy-start | bytes 30724 | tf_op jit(solution)/shard_map/while
  100.8 1.1 copy-start.3
  105.1 3.0 %copy-start.6 = (f32[4,4,160]{2,1,0:T(4,128)S(1)}, f32[4,4,160]{2,1,0:T(4,128)}, u32[]{:S(2)}) copy-start(f32[4,4,160]{2,1,0:T(4,128)} %get-tuple-element.388) | copy-start | bytes 30724 | tf_op jit(solution)/shard_map/while
  105.1 3.1 %copy-start.2 = (f32[4,4,160,128]{3,2,1,0:T(8,128)S(1)}, f32[4,4,160,128]{3,2,1,0:T(8,128)}, u32[]{:S(2)}) copy-start(f32[4,4,160,128]{3,2,1,0:T(8,128)} %get-tuple-element.389) | copy-start | bytes 3932164 | tf_op jit(solution)/shard_map/while
  108.1 2.1 %copy-start.7 = (f32[4,4,160]{2,1,0:T(4,128)}, f32[4,4,160]{2,1,0:T(4,128)S(1)}, u32[]{:S(2)}) copy-start(f32[4,4,160]{2,1,0:T(4,128)S(1)} %get-tuple-element.401) | copy-start | bytes 30724 | tf_op jit(solution)/shard_map/while
  110.2 1.1 copy-start.3
Sparse Core Ops, SparseCore 0:
  10.9 31.2 all-reduce.2
  46.2 22.0 all-gather.4
  70.6 21.7 all-gather.2
  94.6 31.9 reduce-scatter.3
  129.4 21.4 all-reduce.4
where the time goes:
time: 160 us; the launch traced here: 159 us
  waiting for transfers between devices  104 us (65%)
  matrix products  14.8 us (9%)
  between operations  13.9 us (9%)
  local copies, waits for them, and re-layouts  13.8 us (9%)
  other arithmetic  12.3 us (8%)
    psum x1, waiting for transfers between devices, local(): summed = lax.psum(partial_value, 'grp')  31 us
    all_gather x1, waiting for transfers between devices, local(): shard_keys = lax.all_gather(key_rows, 'ctx', axis=0, tiled=True)  24 us
    psum x1, waiting for transfers between devices, local(): replica_total = lax.psum(weight_term.astype(jnp.bfloat16), 'dp')  19.1 us
    unnamed x6, waiting for transfers between devices  15.4 us
    all_gather x1, waiting for transfers between devices, local(): shard_values = lax.all_gather(value_rows, 'ctx', axis=0, tiled=True)  14.4 us
    unnamed x24, local copies, waits for them, and re-layouts  6.19 us
    dot_general x2, matrix products, absorb(): jnp.einsum('kgts,skd->kgtd', weights, value_mat, preferred_element_type=j...  4.06 us
    reduce_sum x2, other arithmetic, absorb(): jnp.sum(weights.astype(jnp.float32), axis=-1)  3.73 us
  transfers between devices with their start and end apart: 5, of which 5 were waited for; matrix products, arithmetic and copies ran while one was open for 18% of the time, Pallas kernels for 0%

commit v1 on v0

v1 whole, which is shorter than its diff:
```python
import functools
import math

import jax
import jax.numpy as jnp
from jax import lax
from jax.experimental import pallas as pl
from jax.experimental.pallas import tpu as pltpu
from jax.sharding import PartitionSpec as P

HEAD_DIM = 128
GROUP_SIZE = 4
MASKED = -2e30
START_MAX = -1e30
EPSILON = 1e-05
F32 = jnp.float32
BF16 = jnp.bfloat16
MESH = pl.DeviceIdType.MESH


def kernel(
    sizes,
    resid_hbm,
    ctx_hbm,
    wo_hbm,
    gain_ref,
    wk_hbm,
    wv_hbm,
    vgrad_hbm,
    lengths_ref,
    query_hbm,
    segment_ref,
    docs_ref,
    cross_ref,
    grad_ref,
    resid_v,
    ctx_v,
    wo_v,
    wk_v,
    wv_v,
    vgrad_v,
    query_v,
    part,
    y_out,
    y_in,
    visual,
    hid_grad,
    stacked,
    k_buf,
    v_buf,
    run_max,
    run_acc,
    scene_col,
    dw,
    dw_core,
    s1,
    dw_x,
    s2,
    dw_z,
    fin,
    fin_in,
    load_sem,
    y_sem,
    vz_sem,
    vy_sem,
    vc_sem,
    dc_sem,
    dx_sem,
    dz_sem,
    df_sem,
):
    n_ctx, n_dp = sizes
    nz = n_ctx // 2
    g = lax.axis_index("grp")
    c = lax.axis_index("ctx")
    r = lax.axis_index("dp")
    z, core = c // 2, c % 2
    half = resid_v.shape[1]
    features = resid_v.shape[2]
    kv_heads = k_buf.shape[0]
    text = query_v.shape[0]
    width = dw.shape[4]
    owner_rows = dw.shape[3]
    chunk = 4 * half

    y_id = (1 - g, c, r)
    core_id = (g, z * 2 + 1 - core, r)

    def z_to(k):
        return lax.rem(z + k, nz)

    def z_from(k):
        return lax.rem(z + nz - k, nz)

    def dp_to(j):
        return lax.rem(r + j, n_dp)

    def dp_from(j):
        return lax.rem(r + n_dp - j, n_dp)

    loads = []
    for i, (src, dst) in enumerate(
        (
            (ctx_hbm, ctx_v),
            (wo_hbm, wo_v),
            (resid_hbm, resid_v),
            (vgrad_hbm, vgrad_v),
            (wk_hbm, wk_v),
            (wv_hbm, wv_v),
            (query_hbm, query_v),
        )
    ):
        load = pltpu.make_async_copy(src, dst, load_sem.at[i])
        load.start()
        loads.append(load)

    barrier = pltpu.get_barrier_semaphore()
    peers = [y_id, core_id]
    peers += [(g, z_to(k) * 2 + core, r) for k in range(1, nz)]
    peers += [(g, c, dp_to(j)) for j in range(1, n_dp)]
    for peer in peers:
        pl.semaphore_signal(barrier, inc=1, device_id=peer, device_id_type=MESH)

    started = []

    def remote(src, dst, sem, device):
        return pltpu.make_async_remote_copy(
            src_ref=src,
            dst_ref=dst,
            send_sem=sem.at[0],
            recv_sem=sem.at[1],
            device_id=device,
            device_id_type=MESH,
        )

    def send(src, dst, sem, device):
        copy = remote(src, dst, sem, device)
        copy.start()
        started.append(copy)

    def arrived(dst, sem, device):
        remote(dst, dst, sem, device).wait_recv()

    loads[0].wait()
    loads[1].wait()
    product = jnp.dot(ctx_v[...], wo_v[...], preferred_element_type=F32)
    part[...] = product.reshape(part.shape)
    y_out[...] = product.astype(BF16).reshape(y_out.shape)
    pl.semaphore_wait(barrier, len(peers))
    for i, h in enumerate((1 - g, g)):
        send(y_out.at[h], y_in.at[h], y_sem.at[i], y_id)

    segment_row = segment_ref[...].astype(F32)
    on_diagonal = lax.broadcasted_iota(jnp.int32, (text, text), 0) == lax.broadcasted_iota(
        jnp.int32, (text, text), 1
    )
    segment_col = jnp.sum(jnp.where(on_diagonal, segment_row, 0.0), axis=1, keepdims=True)
    scene = jnp.zeros((text, 1), F32)
    for d in range(docs_ref.shape[1]):
        scene = scene + jnp.where(segment_col == d, docs_ref[0, d].astype(F32), 0.0)
    scene_col[...] = jnp.broadcast_to(scene, scene_col.shape)

    run_max[...] = jnp.full(run_max.shape, START_MAX, F32)
    run_acc[...] = jnp.zeros(run_acc.shape, F32)
    for head in range(kv_heads):
        v_buf[head, :, HEAD_DIM:] = jnp.ones((chunk, HEAD_DIM), BF16)

    gain = gain_ref[...].astype(F32)
    loads[2].wait()
    loads[3].wait()

    def normalize(h):
        hidden = resid_v[h].astype(F32) + part[h] + y_in[h].astype(F32)
        inverse = lax.rsqrt(jnp.mean(hidden * hidden, axis=-1, keepdims=True) + EPSILON)
        normed = hidden * inverse
        visual[c * 2 + h] = (normed * gain).astype(BF16)
        return normed, inverse

    def backward(h, normed, inverse):
        upstream = vgrad_v[h].astype(F32) * gain
        inner = jnp.mean(upstream * normed, axis=-1, keepdims=True)
        hid_grad[h] = ((upstream - normed * inner) * inverse).astype(BF16)

    arrived(y_in.at[g], y_sem.at[0], y_id)
    saved = normalize(g)
    mine = visual.at[c * 2 + g]
    for k in range(1, nz):
        send(mine, mine, vz_sem.at[k], (g, z_to(k) * 2 + core, r))
    send(mine, mine, vc_sem.at[0, 0], core_id)
    backward(g, *saved)
    arrived(y_in.at[1 - g], y_sem.at[1], y_id)
    saved = normalize(1 - g)
    other = visual.at[c * 2 + 1 - g]
    send(other, other, vc_sem.at[0, 1], core_id)
    backward(1 - g, *saved)

    grads = hid_grad[...].reshape(2 * half, features)
    step = min(HEAD_DIM, ctx_v.shape[1])
    for first in range(0, ctx_v.shape[1], step):
        term = lax.dot_general(
            ctx_v[:, first : first + step],
            grads,
            (((0,), (0,)), ((), ())),
            preferred_element_type=F32,
        ).astype(BF16)
        for low in range(0, step, owner_rows):
            owner = (first + low) // owner_rows
            for j in range(n_dp):
                dw[owner % 2, j, owner // 2] = term[
                    low : low + owner_rows, j * width : (j + 1) * width
                ]
    send(dw.at[1 - core], dw_core, dc_sem, core_id)

    loads[4].wait()
    loads[5].wait()
    loads[6].wait()
    for head in range(kv_heads):
        for member in range(GROUP_SIZE):
            column = (head * GROUP_SIZE + member) * HEAD_DIM
            stacked[head, member * text : (member + 1) * text, :] = query_v[
                :, column : column + HEAD_DIM
            ]

    score_scale = HEAD_DIM ** (-0.5) * math.log2(math.e)

    def absorb(k):
        source = z_from(k)
        mine_id, their_id = source * 2 + core, source * 2 + 1 - core
        arrived(visual.at[their_id * 2 + g], vc_sem.at[k, 0], core_id)
        arrived(visual.at[their_id * 2 + 1 - g], vc_sem.at[k, 1], core_id)
        rows = visual[pl.ds(source * 4, 4)].reshape(chunk, features)
        keys = jnp.dot(rows, wk_v[...], preferred_element_type=F32).astype(BF16)
        values = jnp.dot(rows, wv_v[...], preferred_element_type=F32).astype(BF16)
        for head in range(kv_heads):
            k_buf[head] = keys[:, head * HEAD_DIM : (head + 1) * HEAD_DIM]
            v_buf[head, :, :HEAD_DIM] = values[:, head * HEAD_DIM : (head + 1) * HEAD_DIM]
        position = source * chunk + lax.broadcasted_iota(jnp.int32, (1, chunk), 1)
        key_scene = jnp.zeros((1, chunk), F32)
        end = lengths_ref[0, 0]
        for s in range(lengths_ref.shape[1]):
            key_scene = key_scene + jnp.where(position >= end, 1.0, 0.0)
            if s + 1 < lengths_ref.shape[1]:
                end = end + lengths_ref[0, s + 1]
        allowed = scene_col[:, :1] == key_scene

        def one_head(head):
            scores = lax.dot_general(
                stacked[head], k_buf[head], (((1,), (1,)), ((), ())), preferred_element_type=F32
            )
            scores = scores.reshape(GROUP_SIZE, text, chunk) * score_scale
            scores = jnp.where(allowed[None], scores, MASKED).reshape(GROUP_SIZE * text, chunk)
            old_max = run_max[head][:, :1]
            new_max = jnp.maximum(old_max, jnp.max(scores, axis=1, keepdims=True))
            weights = jnp.exp2(scores - new_max).astype(BF16)
            added = jnp.dot(weights, v_buf[head], preferred_element_type=F32)
            run_acc[head] = run_acc[head] * jnp.exp2(old_max - new_max) + added
            run_max[head] = jnp.broadcast_to(new_max, run_max.shape[1:])

        if nz <= 4:
            for head in range(kv_heads):
                one_head(head)
        else:
            pl.loop(0, kv_heads)(one_head)

    def z_relay(k):
        block = visual.at[(z_from(k) * 2 + core) * 2 + g]
        arrived(block, vz_sem.at[k], y_id)
        send(block, block, vy_sem.at[k], y_id)
        send(block, block, vc_sem.at[k, 0], core_id)

    def y_relay(k):
        block = visual.at[(z_from(k) * 2 + core) * 2 + 1 - g]
        arrived(block, vy_sem.at[k], y_id)
        send(block, block, vc_sem.at[k, 1], core_id)

    def grad_dp():
        arrived(dw_core, dc_sem, core_id)
        s1[...] = (dw[core].astype(F32) + dw_core[...].astype(F32)).astype(BF16)
        for j in range(1, n_dp):
            send(s1.at[dp_to(j)], dw_x.at[j], dx_sem.at[j], (g, c, dp_to(j)))

    def grad_z():
        total = s1[r].astype(F32)
        for j in range(1, n_dp):
            arrived(dw_x.at[j], dx_sem.at[j], (g, c, dp_to(j)))
            total = total + dw_x[j].astype(F32)
        s2[...] = total.astype(BF16)
        for k in range(1, nz):
            send(s2.at[z_to(k)], dw_z.at[k], dz_sem.at[k], (g, z_to(k) * 2 + core, r))

    def grad_final():
        total = s2[z].astype(F32)
        for k in range(1, nz):
            arrived(dw_z.at[k], dz_sem.at[k], (g, z_to(k) * 2 + core, r))
            total = total + dw_z[k].astype(F32)
        fin[...] = total.astype(BF16)
        for j in range(1, n_dp):
            send(fin, fin_in.at[j], df_sem.at[j], (g, c, dp_to(j)))

    grad_dp()
    absorb(0)
    for k in range(1, nz):
        z_relay(k)
        if k == 1:
            grad_z()
        if k >= 2:
            y_relay(k - 1)
        if k >= 3:
            absorb(k - 2)
    y_relay(nz - 1)
    if nz > 2:
        absorb(nz - 2)
    grad_final()
    absorb(nz - 1)

    for head in range(kv_heads):
        result = (run_acc[head][:, :HEAD_DIM] / run_acc[head][:, HEAD_DIM:]).astype(BF16)
        for member in range(GROUP_SIZE):
            column = (head * GROUP_SIZE + member) * HEAD_DIM
            cross_ref[:, column : column + HEAD_DIM] = result[member * text : (member + 1) * text]

    def columns(owner):
        return pl.ds(pl.multiple_of(owner * width, 128), width)

    grad_ref[:, columns(r)] = fin[...].astype(F32)
    for j in range(1, n_dp):
        arrived(fin_in.at[j], df_sem.at[j], (g, c, dp_to(j)))
        grad_ref[:, columns(dp_from(j))] = fin_in[j].astype(F32)

    for copy in started:
        copy.wait_send()


def local(
    n_ctx,
    n_dp,
    resid,
    attn_ctx,
    enc_out_weight,
    enc_gain,
    key_weight,
    value_weight,
    visual_grad,
    scene_lengths,
    text_queries,
    text_segments,
    doc_scene,
):
    rows, features = resid.shape[1:]
    half = rows // 2
    mine = attn_ctx.shape[2]
    text, query_width = text_queries.shape[1:]
    kv_width = key_weight.shape[1]
    kv_heads = kv_width // HEAD_DIM
    nz = n_ctx // 2
    owner_rows = mine // n_ctx
    width = features // n_dp
    chunk = 4 * half
    stacked = GROUP_SIZE * text
    hbm = pl.BlockSpec(memory_space=pl.ANY)
    vmem = pl.BlockSpec(memory_space=pltpu.VMEM)
    smem = pl.BlockSpec(memory_space=pltpu.SMEM)
    sem = pltpu.SemaphoreType.DMA
    halves = (2, half, features)
    cross, grad = pl.pallas_call(
        functools.partial(kernel, (n_ctx, n_dp)),
        out_shape=(
            jax.ShapeDtypeStruct((text, query_width), BF16),
            jax.ShapeDtypeStruct((owner_rows, features), F32),
        ),
        in_specs=[hbm, hbm, hbm, vmem, hbm, hbm, hbm, smem, hbm, vmem, smem],
        out_specs=(vmem, vmem),
        scratch_shapes=[
            pltpu.VMEM(halves, BF16),
            pltpu.VMEM((rows, mine), BF16),
            pltpu.VMEM((mine, features), BF16),
            pltpu.VMEM((features, kv_width), BF16),
            pltpu.VMEM((features, kv_width), BF16),
            pltpu.VMEM(halves, BF16),
            pltpu.VMEM((text, query_width), BF16),
            pltpu.VMEM(halves, F32),
            pltpu.VMEM(halves, BF16),
            pltpu.VMEM(halves, BF16),
            pltpu.VMEM((2 * n_ctx, half, features), BF16),
            pltpu.VMEM(halves, BF16),
            pltpu.VMEM((kv_heads, stacked, HEAD_DIM), BF16),
            pltpu.VMEM((kv_heads, chunk, HEAD_DIM), BF16),
            pltpu.VMEM((kv_heads, chunk, 2 * HEAD_DIM), BF16),
            pltpu.VMEM((kv_heads, stacked, HEAD_DIM), F32),
            pltpu.VMEM((kv_heads, stacked, 2 * HEAD_DIM), F32),
            pltpu.VMEM((text, HEAD_DIM), F32),
            pltpu.VMEM((2, n_dp, nz, owner_rows, width), BF16),
            pltpu.VMEM((n_dp, nz, owner_rows, width), BF16),
            pltpu.VMEM((n_dp, nz, owner_rows, width), BF16),
            pltpu.VMEM((n_dp, nz, owner_rows, width), BF16),
            pltpu.VMEM((nz, owner_rows, width), BF16),
            pltpu.VMEM((nz, owner_rows, width), BF16),
            pltpu.VMEM((owner_rows, width), BF16),
            pltpu.VMEM((n_dp, owner_rows, width), BF16),
            sem((7,)),
            sem((2, 2)),
            sem((nz, 2)),
            sem((nz, 2)),
            sem((nz, 2, 2)),
            sem((2,)),
            sem((n_dp, 2)),
            sem((nz, 2)),
            sem((n_dp, 2)),
        ],
        compiler_params=pltpu.CompilerParams(
            collective_id=0, has_side_effects=True, vmem_limit_bytes=56 * 1024 * 1024
        ),
        name="encoder_cross",
    )(
        resid.reshape(halves),
        attn_ctx.reshape(rows, mine),
        enc_out_weight,
        enc_gain.reshape(1, features),
        key_weight,
        value_weight,
        visual_grad.reshape(halves),
        scene_lengths,
        text_queries.reshape(text, query_width),
        text_segments,
        doc_scene,
    )
    return cross[None], grad


def solution(mesh):
    in_specs = (
        P("dp", "ctx", None),
        P("dp", "ctx", "grp"),
        P("grp", None),
        P(),
        P(None, "grp"),
        P(None, "grp"),
        P("dp", "ctx", None),
        P("dp", None),
        P("dp", "ctx", "grp"),
        P("dp", "ctx"),
        P("dp", None),
    )
    out_specs = (P("dp", "ctx", "grp"), P(("grp", "ctx"), None))
    return jax.shard_map(
        functools.partial(local, mesh.shape["ctx"], mesh.shape["dp"]),
        mesh=mesh,
        in_specs=in_specs,
        out_specs=out_specs,
        check_vma=False,
    )
```

time: 160 us -> 50.1 us (0.31)
  waiting for transfers between devices: 104 us -> 0 us
  Pallas kernels: 0 us -> 45.2 us
  matrix products: 14.8 us -> 0 us
  between operations: 13.9 us -> 0.66 us
  other arithmetic: 12.3 us -> 0 us
  local copies, waits for them, and re-layouts: 13.8 us -> 4 us
    psum x2 -> x0, waiting for transfers between devices: 50.1 us -> none  [the longest x1 31 us: local(): summed = lax.psum(partial_value, 'grp')]
    pallas_call x0 -> x1, Pallas kernels: none -> 45.2 us  [local(): pl.pallas_call(functools.partial(kernel, (n_ctx, n_dp)), out_shape=(jax.S...]
    all_gather x2 -> x0, waiting for transfers between devices: 38.4 us -> none  [the longest x1 24 us: local(): shard_keys = lax.all_gather(key_rows, 'ctx', axis=0, tiled=True)]
    unnamed x6 -> x0, waiting for transfers between devices: 15.4 us -> none
    dot_general x8 -> x0, matrix products: 14.8 us -> none  [the longest x2 4.06 us: absorb(): jnp.einsum('kgts,skd->kgtd', weights, value_mat, preferred_element_type=j...]
    reduce_sum x7 -> x0, other arithmetic: 7.42 us -> none  [the longest x2 3.73 us: absorb(): jnp.sum(weights.astype(jnp.float32), axis=-1)]
    dynamic_slice x6 -> x0, local copies, waits for them, and re-layouts: 3.4 us -> none  [the longest x4 2.98 us: turn_step(): block_values = lax.dynamic_slice_in_dim(shard_values, offset, block, 0)]
    unnamed x24 -> x6, local copies, waits for them, and re-layouts: 6.19 us -> 3.41 us
  transfers between devices with their start and end apart: 5 -> 0, of which waited for: 5 -> 0; matrix products, arithmetic and copies ran while one was open for 18% -> 0% of each run, Pallas kernels for 0% -> 0%
where the time goes in v1:
time: 50.1 us; the launch traced here: 49.8 us
  Pallas kernels  45.2 us (90%)
  local copies, waits for them, and re-layouts  4 us (8%)
  between operations  0.66 us (1%)
    pallas_call x1, Pallas kernels, local(): pl.pallas_call(functools.partial(kernel, (n_ctx, n_dp)), out_shape=(jax.S...  45.2 us
    unnamed x6, local copies, waits for them, and re-layouts  3.41 us

profile of v1, /device:TPU:0, one launch (start us, length us, event | category | flops | bytes accessed | tf_op | source)
XLA Modules:
  0.0 49.8 jit_solution(6838786358181721798)
XLA Ops:
  0.6 0.0 copy-start.1
  0.6 0.7 %copy-done.1 = bf16[1024]{0:T(1024)(128)(2,1)S(1)} copy-done((bf16[1024]{0:T(1024)(128)(2,1)S(1)}, bf16[1024]{0:T(1024)(128)(2,1)}, u32[]{:S(2)}) %copy-start.1) | copy-done | bytes 2072
  1.3 0.6 %reshape.21.gain_ref = bf16[1,1024]{1,0:T(2,128)(2,1)} reshape(bf16[1024]{0:T(1024)(128)(2,1)S(1)} %copy-done.1) | data formatting | bytes 4096 | tf_op jit(solution)/shard_map/reshape | solution.py:418
  1.9 45.2 %encoder_cross.1 = (bf16[160,2048]{1,0:T(8,128)(2,1)}, f32[64,1024]{1,0:T(8,128)}) custom-call(bf16[2,64,1024]{2,1,0:T(8,128)(2,1)} %bitcast.7, bf16[128,512]{1,0:T(8,128)(2,1)} %bitcast.9, bf16[512,1024]{1,0:T(8,128)(2,1)} %wo_hbm.1, bf16[1,1024]{1,0:T(2,128)(2,1)} %reshape.21.gain_ref, bf16[1024,512]{1,0:T(8,128)(2,1)} %wk_hbm.1, ...), custom_call_target="tpu_custom_call" | custom-call | tf_op jit(solution)/shard_map/encoder_cross/pallas_call | solution.py:365
  47.1 0.0 copy-start
  47.1 2.0 %copy.15 = bf16[1,160,2048]{2,1,0:T(8,128)(2,1)} copy(bf16[1,160,2048]{2,1,0:T(8,128)(2,1)} %bitcast.6) | data formatting | bytes 1310720
  49.1 0.0 copy-done
  49.1 0.7 %copy.16 = f32[64,1024]{1,0:T(8,128)} copy(f32[64,1024]{1,0:T(8,128)S(1)} %copy-done) | data formatting | bytes 524288
Async XLA Ops:
  0.6 0.7 %copy-start.1 = (bf16[1024]{0:T(1024)(128)(2,1)S(1)}, bf16[1024]{0:T(1024)(128)(2,1)}, u32[]{:S(2)}) copy-start(bf16[1024]{0:T(1024)(128)(2,1)} %param.14) | copy-start | bytes 6148
  47.1 2.0 %copy-start = (f32[64,1024]{1,0:T(8,128)S(1)}, f32[64,1024]{1,0:T(8,128)}, u32[]{:S(2)}) copy-start(f32[64,1024]{1,0:T(8,128)} %get-tuple-element.9) | copy-start | bytes 786436

commit v2 on v1

--- a/solution.py
+++ b/solution.py
@@ -50,7 +50,8 @@
     v_buf,
     run_max,
     run_acc,
-    scene_col,
+    scene_row,
+    bias,
     dw,
     dw_core,
     s1,
@@ -110,9 +111,9 @@
             (query_hbm, query_v),
         )
     ):
-        load = pltpu.make_async_copy(src, dst, load_sem.at[i])
+        loads.append(pltpu.make_async_copy(src, dst, load_sem.at[i]))
+    for load in loads[:3]:
         load.start()
-        loads.append(load)
 
     barrier = pltpu.get_barrier_semaphore()
     peers = [y_id, core_id]
@@ -143,6 +144,8 @@
 
     loads[0].wait()
     loads[1].wait()
+    for load in loads[3:]:
+        load.start()
     product = jnp.dot(ctx_v[...], wo_v[...], preferred_element_type=F32)
     part[...] = product.reshape(part.shape)
     y_out[...] = product.astype(BF16).reshape(y_out.shape)
@@ -150,22 +153,17 @@
     for i, h in enumerate((1 - g, g)):
         send(y_out.at[h], y_in.at[h], y_sem.at[i], y_id)
 
-    segment_row = segment_ref[...].astype(F32)
-    on_diagonal = lax.broadcasted_iota(jnp.int32, (text, text), 0) == lax.broadcasted_iota(
-        jnp.int32, (text, text), 1
-    )
-    segment_col = jnp.sum(jnp.where(on_diagonal, segment_row, 0.0), axis=1, keepdims=True)
-    scene = jnp.zeros((text, 1), F32)
+    scene = jnp.zeros((1, text), F32)
     for d in range(docs_ref.shape[1]):
-        scene = scene + jnp.where(segment_col == d, docs_ref[0, d].astype(F32), 0.0)
-    scene_col[...] = jnp.broadcast_to(scene, scene_col.shape)
+        scene = scene + jnp.where(segment_ref[...] == d, docs_ref[0, d].astype(F32), 0.0)
+    scene_row[...] = jnp.concatenate([scene] * GROUP_SIZE, axis=1)
 
     run_max[...] = jnp.full(run_max.shape, START_MAX, F32)
     run_acc[...] = jnp.zeros(run_acc.shape, F32)
     for head in range(kv_heads):
-        v_buf[head, :, HEAD_DIM:] = jnp.ones((chunk, HEAD_DIM), BF16)
-
-    gain = gain_ref[...].astype(F32)
+        v_buf[head, HEAD_DIM:, :] = jnp.ones((v_buf.shape[1] - HEAD_DIM, chunk), BF16)
+
+    gain = gain_ref[...].astype(F32).reshape(1, features)
     loads[2].wait()
     loads[3].wait()
 
@@ -230,31 +228,30 @@
         arrived(visual.at[their_id * 2 + 1 - g], vc_sem.at[k, 1], core_id)
         rows = visual[pl.ds(source * 4, 4)].reshape(chunk, features)
         keys = jnp.dot(rows, wk_v[...], preferred_element_type=F32).astype(BF16)
-        values = jnp.dot(rows, wv_v[...], preferred_element_type=F32).astype(BF16)
+        values = jnp.dot(rows, wv_v[...], preferred_element_type=F32).T.astype(BF16)
         for head in range(kv_heads):
             k_buf[head] = keys[:, head * HEAD_DIM : (head + 1) * HEAD_DIM]
-            v_buf[head, :, :HEAD_DIM] = values[:, head * HEAD_DIM : (head + 1) * HEAD_DIM]
-        position = source * chunk + lax.broadcasted_iota(jnp.int32, (1, chunk), 1)
-        key_scene = jnp.zeros((1, chunk), F32)
+            v_buf[head, :HEAD_DIM, :] = values[head * HEAD_DIM : (head + 1) * HEAD_DIM]
+        position = source * chunk + lax.broadcasted_iota(jnp.int32, (chunk, 1), 0)
+        key_scene = jnp.zeros((chunk, 1), F32)
         end = lengths_ref[0, 0]
         for s in range(lengths_ref.shape[1]):
             key_scene = key_scene + jnp.where(position >= end, 1.0, 0.0)
             if s + 1 < lengths_ref.shape[1]:
                 end = end + lengths_ref[0, s + 1]
-        allowed = scene_col[:, :1] == key_scene
+        bias[...] = jnp.where(key_scene == scene_row[...], 0.0, MASKED)
 
         def one_head(head):
             scores = lax.dot_general(
-                stacked[head], k_buf[head], (((1,), (1,)), ((), ())), preferred_element_type=F32
+                k_buf[head], stacked[head], (((1,), (1,)), ((), ())), preferred_element_type=F32
             )
-            scores = scores.reshape(GROUP_SIZE, text, chunk) * score_scale
-            scores = jnp.where(allowed[None], scores, MASKED).reshape(GROUP_SIZE * text, chunk)
-            old_max = run_max[head][:, :1]
-            new_max = jnp.maximum(old_max, jnp.max(scores, axis=1, keepdims=True))
+            scores = scores * score_scale + bias[...]
+            old_max = run_max[head]
+            new_max = jnp.maximum(old_max, jnp.max(scores, axis=0, keepdims=True))
             weights = jnp.exp2(scores - new_max).astype(BF16)
-            added = jnp.dot(weights, v_buf[head], preferred_element_type=F32)
+            added = jnp.dot(v_buf[head], weights, preferred_element_type=F32)
             run_acc[head] = run_acc[head] * jnp.exp2(old_max - new_max) + added
-            run_max[head] = jnp.broadcast_to(new_max, run_max.shape[1:])
+            run_max[head] = new_max
 
         if nz <= 4:
             for head in range(kv_heads):
@@ -314,7 +311,8 @@
     absorb(nz - 1)
 
     for head in range(kv_heads):
-        result = (run_acc[head][:, :HEAD_DIM] / run_acc[head][:, HEAD_DIM:]).astype(BF16)
+        total = run_acc[head]
+        result = (total[:HEAD_DIM] / total[HEAD_DIM : HEAD_DIM + 1]).T.astype(BF16)
         for member in range(GROUP_SIZE):
             column = (head * GROUP_SIZE + member) * HEAD_DIM
             cross_ref[:, column : column + HEAD_DIM] = result[member * text : (member + 1) * text]
@@ -385,10 +383,11 @@
             pltpu.VMEM(halves, BF16),
             pltpu.VMEM((kv_heads, stacked, HEAD_DIM), BF16),
             pltpu.VMEM((kv_heads, chunk, HEAD_DIM), BF16),
-            pltpu.VMEM((kv_heads, chunk, 2 * HEAD_DIM), BF16),
-            pltpu.VMEM((kv_heads, stacked, HEAD_DIM), F32),
-            pltpu.VMEM((kv_heads, stacked, 2 * HEAD_DIM), F32),
-            pltpu.VMEM((text, HEAD_DIM), F32),
+            pltpu.VMEM((kv_heads, HEAD_DIM + 16, chunk), BF16),
+            pltpu.VMEM((kv_heads, 1, stacked), F32),
+            pltpu.VMEM((kv_heads, HEAD_DIM + 16, stacked), F32),
+            pltpu.VMEM((1, stacked), F32),
+            pltpu.VMEM((chunk, stacked), F32),
             pltpu.VMEM((2, n_dp, nz, owner_rows, width), BF16),
             pltpu.VMEM((n_dp, nz, owner_rows, width), BF16),
             pltpu.VMEM((n_dp, nz, owner_rows, width), BF16),
@@ -415,7 +414,7 @@
         resid.reshape(halves),
         attn_ctx.reshape(rows, mine),
         enc_out_weight,
-        enc_gain.reshape(1, features),
+        enc_gain,
         key_weight,
         value_weight,
         visual_grad.reshape(halves),

time: 50.1 us -> 40.2 us (0.80)
  Pallas kernels: 45.2 us -> 36.6 us
  local copies, waits for them, and re-layouts: 4 us -> 2.73 us
    pallas_call x1, Pallas kernels: 45.2 us -> 36.6 us  [local(): pl.pallas_call(functools.partial(kernel, (n_ctx, n_dp)), out_shape=(jax.S...]
    unnamed x6 -> x4, local copies, waits for them, and re-layouts: 3.41 us -> 2.73 us
    reshape x1 -> x0, local copies, waits for them, and re-layouts: 0.6 us -> none  [local(): enc_gain.reshape(1, features)]
where the time goes in v2:
time: 40.2 us; the launch traced here: 40 us
  Pallas kernels  36.6 us (91%)
  local copies, waits for them, and re-layouts  2.73 us (7%)
  between operations  0.65 us (2%)
    pallas_call x1, Pallas kernels, local(): pl.pallas_call(functools.partial(kernel, (n_ctx, n_dp)), out_shape=(jax.S...  36.6 us
    unnamed x4, local copies, waits for them, and re-layouts  2.73 us

profile of v2, /device:TPU:0, one launch (start us, length us, event | category | flops | bytes accessed | tf_op | source)
XLA Modules:
  0.0 40.0 jit_solution(16464881553266225877)
XLA Ops:
  0.6 36.6 %encoder_cross.1 = (bf16[160,2048]{1,0:T(8,128)(2,1)}, f32[64,1024]{1,0:T(8,128)}) custom-call(bf16[2,64,1024]{2,1,0:T(8,128)(2,1)} %bitcast.7, bf16[128,512]{1,0:T(8,128)(2,1)} %bitcast.9, bf16[512,1024]{1,0:T(8,128)(2,1)} %wo_hbm.1, bf16[1024]{0:T(1024)(128)(2,1)} %gain_ref.1, bf16[1024,512]{1,0:T(8,128)(2,1)} %wk_hbm.1, bf16[1024,512]{1,0:T(8,128)(2,1)} %wv_hbm.1, ...), custom_call_target="tpu_custom_call" | custom-call | tf_op jit(solution)/shard_map/encoder_cross/pallas_call | solution.py:363
  37.2 0.0 copy-start
  37.2 2.0 %copy.15 = bf16[1,160,2048]{2,1,0:T(8,128)(2,1)} copy(bf16[1,160,2048]{2,1,0:T(8,128)(2,1)} %bitcast.6) | data formatting | bytes 1310720
  39.3 0.0 copy-done
  39.3 0.7 %copy.16 = f32[64,1024]{1,0:T(8,128)} copy(f32[64,1024]{1,0:T(8,128)S(1)} %copy-done) | data formatting | bytes 524288
Async XLA Ops:
  37.2 2.0 %copy-start = (f32[64,1024]{1,0:T(8,128)S(1)}, f32[64,1024]{1,0:T(8,128)}, u32[]{:S(2)}) copy-start(f32[64,1024]{1,0:T(8,128)} %get-tuple-element.9) | copy-start | bytes 786436
